TPU v7x, 128 devices: a whole 4x4x4 slice. The times are simulated.
128 devices in a mesh: grp: 4 (over z), dp: 32 (over x, y, core).
Axes of the slice: x: 4, y: 4, z: 4, core: 2. Of those that a mesh axis runs over, the one named last changes fastest.
Arguments:
- caption_token_index: int32 [32, 64], P('dp'), may hold values from 0 to 32767
- lengths: int32 [32], P('dp'), may hold values from 1 to 64
- slot_image_pair: int32 [32], P('dp'), may hold values from 0 to 31, each once
- features: bfloat16 [32, 256, 1024], P('dp'), may hold values from -6 to 6
- text_table: bfloat16 [32768, 2048], P(('grp', 'dp')), may hold values from -6 to 6
- latents: bfloat16 [64, 2048], P(None, 'dp'), may hold values from -6 to 6
- sampler_gain: bfloat16 [2048], P('dp'), may hold values from 0.099609375 to 1.8984375
- sampler_query: bfloat16 [2048, 2048], P('dp', 'grp'), may hold values from -0.125 to 0.125
- sampler_source: bfloat16 [1024, 2, 2048], P('dp', None, 'grp'), may hold values from -0.25 to 0.25
- sampler_mixer: bfloat16 [2048, 2048], P('grp', 'dp'), may hold values from -1 to 1
- norm_gain_one: bfloat16 [2048], P('dp'), may hold values from 0.099609375 to 1.8984375
- attention_in: bfloat16 [2048, 3, 2048], P('dp', None, 'grp'), may hold values from -0.1875 to 0.1875
- norm_gain_two: bfloat16 [2048], P(('grp', 'dp')), may hold values from 0.099609375 to 1.8984375
- attention_out: bfloat16 [2048, 2048], P('grp', 'dp'), may hold values from -0.125 to 0.125
- norm_gain_three: bfloat16 [2048], P('dp'), may hold values from 0.099609375 to 1.8984375
- feed_up: bfloat16 [2048, 8192], P('dp', 'grp'), may hold values from -0.125 to 0.125
- norm_gain_four: bfloat16 [8192], P(('grp', 'dp')), may hold values from 0.099609375 to 1.8984375
- feed_down: bfloat16 [8192, 2048], P('grp', 'dp'), may hold values from -0.0625 to 0.0625
- cotangent: bfloat16 [32, 128, 2048], P('dp'), may hold values from -6 to 6
Outputs:
- layer_output: float32 [32, 128, 2048], P('dp')
- input_grad: float32 [32, 128, 2048], P('dp')
- table_grad: float32 [32768, 2048], P(('grp', 'dp'))
- latents_grad: float32 [64, 2048], P(None, 'dp')
- sampler_gain_grad: float32 [2048], P('dp')
- sampler_query_grad: float32 [2048, 2048], P('dp', 'grp')
- sampler_source_grad: float32 [1024, 2, 2048], P('dp', None, 'grp')
- sampler_mixer_grad: float32 [2048, 2048], P('grp', 'dp')
- gain_one_grad: float32 [2048], P('dp')
- attention_in_grad: float32 [2048, 3, 2048], P('dp', None, 'grp')
- gain_two_grad: float32 [2048], P(('grp', 'dp'))
- attention_out_grad: float32 [2048, 2048], P('grp', 'dp')
- gain_three_grad: float32 [2048], P('dp')
- feed_up_grad: float32 [2048, 8192], P('dp', 'grp')
- gain_four_grad: float32 [8192], P(('grp', 'dp'))
- feed_down_grad: float32 [8192, 2048], P('grp', 'dp')
Inputs may be any that keep to these rules, and one draw needn't show every extreme that they name: `slot_image_pair`: every pair fills exactly one slot.
All inputs are finite; a program needn't handle non-finite values.
Results may differ from a plain program's by a relative error of at most 0.025.
The roundings to bfloat16 on the way count: a program that leaves them out, or rounds other values in their place, can miss the bound.
Values may be sent and summed in bfloat16 or wider, within the bound.
No kernel may reach another device: no remote copies, remote signals or barrier semaphores. Data moves between devices by JAX's collectives and lax.ppermute only.
A program may use at most 512 MiB of HBM per device.

v0:
```python
from functools import partial

import jax
import jax.numpy as jnp
from jax import lax
from jax.sharding import PartitionSpec as P

MODEL_WIDTH = 2048
HD = 64
FF = 8192
PATCH_COUNT = 256
NL = 64
RHD = 128
SLOT_TOKENS = 128
CAPTION_SPAN = 64


EPSILON = 1e-05
NEG_FILL = -1e30


def layer_norm(values, scale_gain):
    center = values - jnp.mean(values, axis=-1, keepdims=True)
    spread = jnp.mean(center * center, axis=-1, keepdims=True)
    return center * lax.rsqrt(spread + EPSILON) * scale_gain


def head_total(partial_sum):
    return lax.psum(partial_sum, "grp")


def row_total(partial_rows):
    return lax.psum(partial_rows, "grp")


def split_norm(values, full_width):
    mean_rows = row_total(jnp.sum(values, axis=-1, keepdims=True)) / full_width
    center = values - mean_rows
    spread = row_total(jnp.sum(center * center, axis=-1, keepdims=True)) / full_width
    scale_rows = lax.rsqrt(spread + EPSILON)
    return (center * scale_rows, scale_rows)


def split_norm_back(grad_normed, normed, scale_rows, scale_gain, full_width):
    grad_hat = grad_normed * scale_gain.astype(jnp.float32)
    sum_grad, sum_cross = row_total(
        (
            jnp.sum(grad_hat, axis=-1, keepdims=True),
            jnp.sum(grad_hat * normed, axis=-1, keepdims=True),
        )
    )
    grad_values = scale_rows * (
        grad_hat - sum_grad / full_width - normed * (sum_cross / full_width)
    )
    grad_gain = jnp.sum(grad_normed * normed, axis=0)
    return (grad_values, grad_gain)


def pick_rows(slot_image_pair):

    def picker(current, shard_rows, first_row):
        span_rows = shard_rows.shape[0]
        inside = (slot_image_pair >= 0) & (slot_image_pair < span_rows)
        picked = jnp.take(shard_rows, jnp.clip(slot_image_pair, 0, span_rows - 1), axis=0)
        return jnp.where(inside[:, None, None], picked, current)

    return picker


def image_term(slot_image_pair, grad_source, span_rows):
    pair_ids = jnp.arange(span_rows, dtype=jnp.int32)
    matches = (pair_ids[:, None] == slot_image_pair[None, :]).astype(jnp.float32)
    return jnp.einsum("cs,snd->cnd", matches, grad_source, precision=lax.Precision.HIGHEST)


def shards(
    caption_token_index,
    lengths,
    slot_image_pair,
    features,
    text_table,
    latents,
    sampler_gain,
    sampler_query,
    sampler_source,
    sampler_mixer,
    norm_gain_one,
    attention_in,
    norm_gain_two,
    attention_out,
    norm_gain_three,
    feed_up,
    norm_gain_four,
    feed_down,
    cotangent,
):
    group_index = lax.axis_index("grp")
    slot_count = caption_token_index.shape[0]
    pair_count = features.shape[0]
    latent_rows, query_gain, query_weight, source_weight, mixer_weight = (
        lax.all_gather(latents, "dp", axis=1, tiled=True),
        lax.all_gather(sampler_gain, "dp", axis=0, tiled=True),
        lax.all_gather(sampler_query, "dp", axis=0, tiled=True),
        lax.all_gather(sampler_source, "dp", axis=0, tiled=True),
        lax.all_gather(sampler_mixer, "dp", axis=1, tiled=True),
    )
    latent_values = latent_rows.astype(jnp.float32)
    query_norm, query_back = jax.vjp(layer_norm, latent_values, query_gain.astype(jnp.float32))
    query_input = query_norm.astype(jnp.bfloat16)
    local_heads = query_weight.shape[1] // RHD
    query_heads = (
        jnp.dot(query_input, query_weight, preferred_element_type=jnp.float32)
        .astype(jnp.bfloat16)
        .reshape(NL, local_heads, RHD)
    )
    sources = jnp.einsum(
        "pnf,fce->pnce", features, source_weight, preferred_element_type=jnp.float32
    ).astype(jnp.bfloat16)
    key_heads = sources[:, :, 0].reshape(pair_count, PATCH_COUNT, local_heads, RHD)
    value_heads = sources[:, :, 1].reshape(pair_count, PATCH_COUNT, local_heads, RHD)
    sampler_factor = RHD ** (-0.5)
    scores = (
        jnp.einsum("lhe,pnhe->phln", query_heads, key_heads, preferred_element_type=jnp.float32)
        * sampler_factor
    )
    maxima = jnp.max(scores, axis=-1, keepdims=True)
    exponent = jnp.exp(scores - maxima)
    totals = jnp.sum(exponent, axis=-1, keepdims=True)
    sampler_log = maxima + jnp.log(totals)
    weights = (exponent / totals).astype(jnp.bfloat16)
    attended = jnp.einsum(
        "phln,pnhe->plhe", weights, value_heads, preferred_element_type=jnp.float32
    )
    attended = attended.reshape(pair_count, NL, local_heads * RHD).astype(jnp.bfloat16)
    mixed_part = jnp.einsum(
        "pld,de->ple", attended, mixer_weight, preferred_element_type=jnp.float32
    )
    embedded = (latent_values[None] + head_total(mixed_part)).astype(jnp.bfloat16)
    picker = pick_rows(slot_image_pair)
    image_rows = picker(
        jnp.zeros((slot_count, NL, MODEL_WIDTH), jnp.bfloat16),
        lax.all_gather(embedded, "dp", axis=0, tiled=True),
        jnp.int32(0),
    )
    quarter = text_table.shape[0] * lax.axis_size("dp")
    vocab_base = group_index * quarter
    flat_ids = caption_token_index.reshape(-1)
    shard_rows = lax.all_gather(text_table, "dp", axis=0, tiled=True)
    span_rows = shard_rows.shape[0]
    columns = vocab_base + jnp.arange(span_rows, dtype=jnp.int32)
    one_hot = (flat_ids[:, None] == columns[None, :]).astype(jnp.bfloat16)
    text_part = jnp.dot(one_hot, shard_rows, preferred_element_type=jnp.float32)
    text_rows = head_total(text_part).reshape(slot_count, CAPTION_SPAN, MODEL_WIDTH)
    inputs = jnp.concatenate([image_rows.astype(jnp.float32), text_rows], axis=1)
    norm_one, attn_weight, norm_two, out_weight, norm_three, up_weight, norm_four, down_weight = (
        lax.all_gather(norm_gain_one, "dp", axis=0, tiled=True),
        lax.all_gather(attention_in, "dp", axis=0, tiled=True),
        lax.all_gather(norm_gain_two, "dp", axis=0, tiled=True),
        lax.all_gather(attention_out, "dp", axis=1, tiled=True),
        lax.all_gather(norm_gain_three, "dp", axis=0, tiled=True),
        lax.all_gather(feed_up, "dp", axis=0, tiled=True),
        lax.all_gather(norm_gain_four, "dp", axis=0, tiled=True),
        lax.all_gather(feed_down, "dp", axis=1, tiled=True),
    )
    rows_flat = inputs.reshape(slot_count * SLOT_TOKENS, MODEL_WIDTH)
    first_norm, first_back = jax.vjp(layer_norm, rows_flat, norm_one.astype(jnp.float32))
    first_input = first_norm.astype(jnp.bfloat16)
    projected = jnp.einsum(
        "td,dce->tce", first_input, attn_weight, preferred_element_type=jnp.float32
    ).astype(jnp.bfloat16)
    heads_here = attn_weight.shape[2] // HD
    shape_heads = (slot_count, SLOT_TOKENS, heads_here, HD)
    query_text = projected[:, 0].reshape(shape_heads)
    key_text = projected[:, 1].reshape(shape_heads)
    value_text = projected[:, 2].reshape(shape_heads)
    positions = jnp.arange(SLOT_TOKENS, dtype=jnp.int32)
    causal = (positions[None, :] <= positions[:, None])[None, None]
    allowed = causal & (positions[None, None, None, :] < NL + lengths[:, None, None, None])
    text_factor = HD ** (-0.5)

    def masked_scores():
        raw = (
            jnp.einsum("bqhe,bkhe->bhqk", query_text, key_text, preferred_element_type=jnp.float32)
            * text_factor
        )
        return jnp.where(allowed, raw, NEG_FILL)

    scores = masked_scores()
    maxima = jnp.max(scores, axis=-1, keepdims=True)
    exponent = jnp.exp(scores - maxima)
    totals = jnp.sum(exponent, axis=-1, keepdims=True)
    text_log = maxima + jnp.log(totals)
    weights = (exponent / totals).astype(jnp.bfloat16)
    attended_text = jnp.einsum(
        "bhqk,bkhe->bqhe", weights, value_text, preferred_element_type=jnp.float32
    )
    attended_text = attended_text.reshape(slot_count * SLOT_TOKENS, heads_here * HD)
    second_hat, second_scale = split_norm(attended_text, MODEL_WIDTH)
    second_input = (second_hat * norm_two.astype(jnp.float32)).astype(jnp.bfloat16)
    branch = head_total(jnp.dot(second_input, out_weight, preferred_element_type=jnp.float32))
    middle = rows_flat + branch
    third_norm, third_back = jax.vjp(layer_norm, middle, norm_three.astype(jnp.float32))
    third_input = third_norm.astype(jnp.bfloat16)
    up_rows = jnp.dot(third_input, up_weight, preferred_element_type=jnp.float32)
    activated, gelu_back = jax.vjp(partial(jax.nn.gelu, approximate=False), up_rows)
    fourth_hat, fourth_scale = split_norm(activated, FF)
    fourth_input = (fourth_hat * norm_four.astype(jnp.float32)).astype(jnp.bfloat16)
    result = middle + head_total(
        jnp.dot(fourth_input, down_weight, preferred_element_type=jnp.float32)
    )
    layer_output = result.reshape(slot_count, SLOT_TOKENS, MODEL_WIDTH)
    grad_output = cotangent.reshape(slot_count * SLOT_TOKENS, MODEL_WIDTH)
    grad_down = jnp.einsum(
        "tf,td->fd", fourth_input, grad_output, preferred_element_type=jnp.float32
    )
    grad_fourth = jnp.einsum(
        "td,fd->tf", grad_output, down_weight, preferred_element_type=jnp.float32
    )
    grad_active, grad_norm_four = split_norm_back(
        grad_fourth, fourth_hat, fourth_scale, norm_four, FF
    )
    grad_up_rows = gelu_back(grad_active)[0].astype(jnp.bfloat16)
    grad_up = jnp.einsum("td,tf->df", third_input, grad_up_rows, preferred_element_type=jnp.float32)
    grad_third = head_total(
        jnp.einsum("tf,df->td", grad_up_rows, up_weight, preferred_element_type=jnp.float32)
    )
    grad_mid_norm, grad_norm_three = third_back(grad_third)
    grad_middle = grad_output.astype(jnp.float32) + grad_mid_norm
    grad_branch_low = grad_middle.astype(jnp.bfloat16)
    grad_out_weight = jnp.einsum(
        "td,te->de", second_input, grad_branch_low, preferred_element_type=jnp.float32
    )
    grad_second = jnp.einsum(
        "te,de->td", grad_branch_low, out_weight, preferred_element_type=jnp.float32
    )
    grad_attended, grad_norm_two = split_norm_back(
        grad_second, second_hat, second_scale, norm_two, MODEL_WIDTH
    )
    grad_att_low = grad_attended.astype(jnp.bfloat16).reshape(shape_heads)
    probability = jnp.exp(masked_scores() - text_log)
    weights_low = probability.astype(jnp.bfloat16)
    grad_value = jnp.einsum(
        "bhqk,bqhe->bkhe", weights_low, grad_att_low, preferred_element_type=jnp.float32
    )
    grad_weights = jnp.einsum(
        "bqhe,bkhe->bhqk", grad_att_low, value_text, preferred_element_type=jnp.float32
    )
    grad_scores = probability * (
        grad_weights - jnp.sum(probability * grad_weights, axis=-1, keepdims=True)
    )
    grad_scores = grad_scores.astype(jnp.bfloat16)
    grad_query = (
        jnp.einsum("bhqk,bkhe->bqhe", grad_scores, key_text, preferred_element_type=jnp.float32)
        * text_factor
    )
    grad_key = (
        jnp.einsum("bhqk,bqhe->bkhe", grad_scores, query_text, preferred_element_type=jnp.float32)
        * text_factor
    )
    flat_shape = (slot_count * SLOT_TOKENS, heads_here * HD)
    grad_projected = jnp.stack(
        [
            grad_query.reshape(flat_shape),
            grad_key.reshape(flat_shape),
            grad_value.reshape(flat_shape),
        ],
        axis=1,
    ).astype(jnp.bfloat16)
    grad_attn_weight = jnp.einsum(
        "td,tce->dce", first_input, grad_projected, preferred_element_type=jnp.float32
    )
    grad_first = head_total(
        jnp.einsum("tce,dce->td", grad_projected, attn_weight, preferred_element_type=jnp.float32)
    )
    grad_in_norm, grad_norm_one = first_back(grad_first)
    input_grad = (grad_middle + grad_in_norm).reshape(slot_count, SLOT_TOKENS, MODEL_WIDTH)
    text_low = lax.optimization_barrier(
        input_grad[:, NL:].reshape(slot_count * CAPTION_SPAN, MODEL_WIDTH).astype(jnp.bfloat16)
    ).astype(jnp.float32)
    span_rows = text_table.shape[0] * lax.axis_size("dp")
    local_ids = flat_ids - vocab_base
    inside = (local_ids >= 0) & (local_ids < span_rows)
    summed = jax.ops.segment_sum(
        text_low, jnp.where(inside, local_ids, span_rows), num_segments=span_rows + 1
    )
    table_grad = lax.psum_scatter(summed[:span_rows], "dp", scatter_dimension=0, tiled=True)
    grad_image = input_grad[:, :NL]
    grad_embedded = lax.psum_scatter(
        image_term(slot_image_pair, grad_image, pair_count * lax.axis_size("dp")),
        "dp",
        scatter_dimension=0,
        tiled=True,
    ).astype(jnp.bfloat16)
    grad_latent_direct = jnp.sum(grad_embedded.astype(jnp.float32), axis=0)
    grad_mixer = jnp.einsum(
        "pld,ple->de", attended, grad_embedded, preferred_element_type=jnp.float32
    )
    grad_sampled = jnp.einsum(
        "ple,de->pld", grad_embedded, mixer_weight, preferred_element_type=jnp.float32
    )
    grad_sampled = grad_sampled.astype(jnp.bfloat16).reshape(pair_count, NL, local_heads, RHD)
    sampler_scores = (
        jnp.einsum("lhe,pnhe->phln", query_heads, key_heads, preferred_element_type=jnp.float32)
        * sampler_factor
    )
    sampler_prob = jnp.exp(sampler_scores - sampler_log)
    sampler_low = sampler_prob.astype(jnp.bfloat16)
    grad_source_value = jnp.einsum(
        "phln,plhe->pnhe", sampler_low, grad_sampled, preferred_element_type=jnp.float32
    )
    grad_sampler_weights = jnp.einsum(
        "plhe,pnhe->phln", grad_sampled, value_heads, preferred_element_type=jnp.float32
    )
    grad_sampler_scores = sampler_prob * (
        grad_sampler_weights - jnp.sum(sampler_prob * grad_sampler_weights, axis=-1, keepdims=True)
    )
    grad_sampler_scores = grad_sampler_scores.astype(jnp.bfloat16)
    grad_query_heads = (
        jnp.einsum(
            "phln,pnhe->lhe", grad_sampler_scores, key_heads, preferred_element_type=jnp.float32
        )
        * sampler_factor
    )
    grad_source_key = (
        jnp.einsum(
            "phln,lhe->pnhe", grad_sampler_scores, query_heads, preferred_element_type=jnp.float32
        )
        * sampler_factor
    )
    source_shape = (pair_count, PATCH_COUNT, local_heads * RHD)
    grad_sources = jnp.stack(
        [grad_source_key.reshape(source_shape), grad_source_value.reshape(source_shape)], axis=2
    ).astype(jnp.bfloat16)
    grad_source_weight = jnp.einsum(
        "pnf,pnce->fce", features, grad_sources, preferred_element_type=jnp.float32
    )
    grad_query_low = grad_query_heads.reshape(NL, local_heads * RHD).astype(jnp.bfloat16)
    grad_query_weight = jnp.einsum(
        "ld,le->de", query_input, grad_query_low, preferred_element_type=jnp.float32
    )
    grad_query_input = head_total(
        jnp.einsum("le,de->ld", grad_query_low, query_weight, preferred_element_type=jnp.float32)
    )
    grad_latent_norm, grad_query_gain = query_back(grad_query_input)
    grad_latent = grad_latent_direct + grad_latent_norm
    sampler_grads = (
        lax.psum_scatter(grad_latent, "dp", scatter_dimension=1, tiled=True),
        lax.psum_scatter(grad_query_gain, "dp", scatter_dimension=0, tiled=True),
        lax.psum_scatter(grad_query_weight, "dp", scatter_dimension=0, tiled=True),
        lax.psum_scatter(grad_source_weight, "dp", scatter_dimension=0, tiled=True),
        lax.psum_scatter(grad_mixer, "dp", scatter_dimension=1, tiled=True),
    )
    layer_grads = (
        lax.psum_scatter(grad_norm_one, "dp", scatter_dimension=0, tiled=True),
        lax.psum_scatter(grad_attn_weight, "dp", scatter_dimension=0, tiled=True),
        lax.psum_scatter(grad_norm_two, "dp", scatter_dimension=0, tiled=True),
        lax.psum_scatter(grad_out_weight, "dp", scatter_dimension=1, tiled=True),
        lax.psum_scatter(grad_norm_three, "dp", scatter_dimension=0, tiled=True),
        lax.psum_scatter(grad_up, "dp", scatter_dimension=0, tiled=True),
        lax.psum_scatter(grad_norm_four, "dp", scatter_dimension=0, tiled=True),
        lax.psum_scatter(grad_down, "dp", scatter_dimension=1, tiled=True),
    )
    return (
        layer_output,
        input_grad,
        table_grad,
        sampler_grads[0],
        sampler_grads[1],
        sampler_grads[2],
        sampler_grads[3],
        sampler_grads[4],
        layer_grads[0],
        layer_grads[1],
        layer_grads[2],
        layer_grads[3],
        layer_grads[4],
        layer_grads[5],
        layer_grads[6],
        layer_grads[7],
    )


def solution(mesh):
    return jax.shard_map(
        shards,
        mesh=mesh,
        in_specs=(
            P("dp", None),
            P("dp"),
            P("dp"),
            P("dp", None, None),
            P(("grp", "dp"), None),
            P(None, "dp"),
            P("dp"),
            P("dp", "grp"),
            P("dp", None, "grp"),
            P("grp", "dp"),
            P("dp"),
            P("dp", None, "grp"),
            P(("grp", "dp")),
            P("grp", "dp"),
            P("dp"),
            P("dp", "grp"),
            P(("grp", "dp")),
            P("grp", "dp"),
            P("dp", None, None),
        ),
        out_specs=(
            P("dp", None, None),
            P("dp", None, None),
            P(("grp", "dp"), None),
            P(None, "dp"),
            P("dp"),
            P("dp", "grp"),
            P("dp", None, "grp"),
            P("grp", "dp"),
            P("dp"),
            P("dp", None, "grp"),
            P(("grp", "dp")),
            P("grp", "dp"),
            P("dp"),
            P("dp", "grp"),
            P(("grp", "dp")),
            P("grp", "dp"),
        ),
        check_vma=False,
    )
```

profile of v0, /device:TPU:0, one launch (start us, length us, event | category | flops | bytes accessed | tf_op | source)
XLA Modules:
  0.0 2091.3 jit_solution(7970596985159569377)
XLA Ops:
  17.8 128.9 %all-reduce.16 = (bf16[2048]{0:T(1024)(128)(2,1)S(1)}, bf16[2048]{0:T(1024)(128)(2,1)S(1)}, bf16[512]{0:T(512)(128)(2,1)S(1)}, bf16[2048]{0:T(1024)(128)(2,1)S(1)}, bf16[2048]{0:T(1024)(128)(2,1)S(1)}) all-reduce(bf16[2048]{0:T(1024)(128)(2,1)S(1)} %dynamic-update-slice.2, ...), channel_id=1, replica_groups=mesh['grp'=4,'dp'=32] {'dp'}, use_global_device_ids=true, to_apply=%add.1 | all-reduce | flops 8704 | bytes 34816
  147.5 22.0 %all_gather.45 = bf16[64,2048]{0,1:T(8,128)(2,1)S(1)} all-gather(bf16[64,64]{0,1:T(8,128)(2,1)S(1)} %copy.87), channel_id=1, replica_groups=mesh['grp'=4,'dp'=32] {'dp'}, dimensions={1}, use_global_device_ids=true | all-gather | bytes 270336 | tf_op jit(solution)/shard_map/all_gather | solution.py:101
  180.6 82.7 %all-gather.18.cloned.1.call-done = bf16[8192,2048]{1,0:T(8,128)(2,1)} async-done(((bf16[256,2048]{1,0:T(8,128)(2,1)}), bf16[8192,2048]{1,0:T(8,128)(2,1)}) %all-gather.18.cloned.1.call-update) | async-done | bytes 33554448 | tf_op jit(solution)/shard_map/all_gather | solution.py:148
  277.8 45.6 %all-reduce.34.cloned.1.call-done = (f32[1,64,2048]{2,1,0:T(8,128)}, f32[1,64,2048]{2,1,0:T(8,128)}) async-done(((f32[1,64,2048]{2,1,0:T(8,128)}, f32[1,64,2048]{2,1,0:T(8,128)}), (f32[1,64,2048]{2,1,0:T(8,128)}, f32[1,64,2048]{2,1,0:T(8,128)})) %all-reduce.34.cloned.1.call-update) | async-done | bytes 1048592 | tf_op jit(solution)/shard_map/psum | solution.py:29
  328.3 51.7 %all-gather.16.cloned.1.call-done = bf16[32,64,2048]{2,1,0:T(8,128)(2,1)} async-done(((bf16[1,64,2048]{2,1,0:T(8,128)(2,1)}), bf16[32,64,2048]{2,1,0:T(8,128)(2,1)}) %all-gather.16.cloned.1.call-update) | async-done | bytes 8388624 | tf_op jit(solution)/shard_map/all_gather | solution.py:142
  383.5 47.8 %all-gather.20.cloned.1.call-done = bf16[2048,3,512]{2,0,1:T(8,128)(2,1)} async-done(((bf16[64,3,512]{2,0,1:T(8,128)(2,1)}), bf16[2048,3,512]{2,0,1:T(8,128)(2,1)}) %all-gather.20.cloned.1.call-update) | async-done | bytes 6291472 | tf_op jit(solution)/shard_map/all_gather | solution.py:157
  455.3 21.2 %all-gather.22.cloned.1.call-done = bf16[512,2048]{0,1:T(8,128)(2,1)} async-done(((bf16[512,64]{0,1:T(8,128)(2,1)}), bf16[512,2048]{0,1:T(8,128)(2,1)}) %all-gather.22.cloned.1.call-update) | async-done | bytes 2097168 | tf_op jit(solution)/shard_map/all_gather | solution.py:159
  482.1 43.4 %all-reduce.24.cloned.1.call-done = f32[128,2048]{1,0:T(8,128)} async-done(((f32[128,2048]{1,0:T(8,128)}), f32[128,2048]{1,0:T(8,128)}) %all-reduce.24.cloned.1.call-update) | async-done | bytes 1048592 | tf_op jit(solution)/shard_map/psum | solution.py:29
  527.8 53.2 %all-gather.24.cloned.1.call-done = bf16[2048,2048]{1,0:T(8,128)(2,1)} async-done(((bf16[64,2048]{1,0:T(8,128)(2,1)}), bf16[2048,2048]{1,0:T(8,128)(2,1)}) %all-gather.24.cloned.1.call-update) | async-done | bytes 8388624 | tf_op jit(solution)/shard_map/all_gather | solution.py:161
  612.4 23.3 %all-gather.26.cloned.1.call-done = bf16[2048,2048]{0,1:T(8,128)(2,1)} async-done(((bf16[2048,64]{0,1:T(8,128)(2,1)}), bf16[2048,2048]{0,1:T(8,128)(2,1)}) %all-gather.26.cloned.1.call-update) | async-done | bytes 8388624 | tf_op jit(solution)/shard_map/all_gather | solution.py:163
  666.4 42.3 %all-reduce.26.cloned.1.call-done = f32[128,2048]{1,0:T(8,128)} async-done(((f32[128,2048]{1,0:T(8,128)}), f32[128,2048]{1,0:T(8,128)}) %all-reduce.26.cloned.1.call-update) | async-done | bytes 1048592 | tf_op jit(solution)/shard_map/psum | solution.py:29
  750.8 44.7 %all-reduce.28.cloned.1.call-done = f32[128,2048]{1,0:T(8,128)} async-done(((f32[128,2048]{1,0:T(8,128)}), f32[128,2048]{1,0:T(8,128)}) %all-reduce.28.cloned.1.call-update) | async-done | bytes 1048592 | tf_op jit(solution)/shard_map/psum | solution.py:29
  819.6 107.2 %reduce-scatter.14.cloned.1.call-done = f32[1,64,2048]{2,1,0:T(8,128)} async-done(((f32[32,64,2048]{2,1,0:T(8,128)}), f32[1,64,2048]{2,1,0:T(8,128)}) %reduce-scatter.14.cloned.1.call-update) | async-done | bytes 524304 | tf_op jit(solution)/shard_map/reduce_scatter | solution.py:288
  949.6 37.9 %all-reduce.32.cloned.1.call-done = (f32[128,2048]{1,0:T(8,128)}, f32[64,2048]{1,0:T(8,128)}) async-done(((f32[128,2048]{1,0:T(8,128)}, f32[64,2048]{1,0:T(8,128)}), (f32[128,2048]{1,0:T(8,128)}, f32[64,2048]{1,0:T(8,128)})) %all-reduce.32.cloned.1.call-update) | async-done | bytes 1572880 | tf_op jit(solution)/shard_map/psum | solution.py:29
  1034.3 21.3 %broadcast_in_dim.141 = f32[8193,2048]{1,0:T(8,128)} broadcast(f32[]{:T(128)} %constant.56.clone.1), dimensions={} | broadcast | bytes 67117056 | tf_op jit(solution)/shard_map/broadcast_in_dim | solution.py:283
  1068.6 44.0 %slice.48 = f32[8192,2048]{1,0:T(8,128)} slice(f32[8193,2048]{1,0:T(8,128)} %scatter_fusion), slice={[0:8192], [0:2048]} | slice | bytes 134217728 | tf_op jit(solution)/shard_map/slice | solution.py:286
  1114.8 129.6 %all-reduce.11 = (f32[2048]{0:T(1024)S(1)}, f32[2048]{0:T(1024)S(1)}, f32[512]{0:T(512)S(1)}, f32[2048]{0:T(1024)S(1)}, f32[2048]{0:T(1024)S(1)}) all-reduce(f32[2048]{0:T(1024)S(1)} %copy-done.37, f32[2048]{0:T(1024)S(1)} %copy-done.36, f32[512]{0:T(512)S(1)} %copy-done.55, ...), channel_id=5, replica_groups=mesh['grp'=4,'dp'=32] {'dp'}, use_global_device_ids=true, to_apply=%region_46.47.clone | all-reduce | flops 8704 | bytes 69632
  1251.4 16.9 reduce-scatter.22.cloned.1.call-done
  1268.4 108.1 %reduce-scatter.20.cloned.1.call-done = f32[64,3,512]{2,0,1:T(8,128)} async-done(((f32[2048,3,512]{2,0,1:T(8,128)}), f32[64,3,512]{2,0,1:T(8,128)}) %reduce-scatter.20.cloned.1.call-update) | async-done | bytes 393232 | tf_op jit(solution)/shard_map/reduce_scatter | solution.py:355
  1376.4 119.3 %reduce-scatter.26.cloned.1.call-done = f32[2048,64]{0,1:T(8,128)} async-done(((f32[2048,2048]{0,1:T(8,128)}), f32[2048,64]{0,1:T(8,128)}) %reduce-scatter.26.cloned.1.call-update) | async-done | bytes 524304 | tf_op jit(solution)/shard_map/reduce_scatter | solution.py:361
  1495.7 119.5 %reduce-scatter.24.cloned.1.call-done = f32[64,2048]{1,0:T(8,128)} async-done(((f32[2048,2048]{1,0:T(8,128)}), f32[64,2048]{1,0:T(8,128)}) %reduce-scatter.24.cloned.1.call-update) | async-done | bytes 524304 | tf_op jit(solution)/shard_map/reduce_scatter | solution.py:359
  1615.3 85.9 %reduce-scatter.18.cloned.1.call-done = f32[512,64]{0,1:T(8,128)} async-done(((f32[512,2048]{0,1:T(8,128)}), f32[512,64]{0,1:T(8,128)}) %reduce-scatter.18.cloned.1.call-update) | async-done | bytes 131088 | tf_op jit(solution)/shard_map/reduce_scatter | solution.py:351
  1701.2 85.4 %reduce-scatter.16.cloned.1.call-done = f32[64,512]{1,0:T(8,128)} async-done(((f32[2048,512]{1,0:T(8,128)}), f32[64,512]{1,0:T(8,128)}) %reduce-scatter.16.cloned.1.call-update) | async-done | bytes 131088 | tf_op jit(solution)/shard_map/reduce_scatter | solution.py:349
  1786.6 297.4 %reduce-scatter.12.cloned.1.call-done = f32[256,2048]{1,0:T(8,128)} async-done(((f32[8192,2048]{1,0:T(8,128)}), f32[256,2048]{1,0:T(8,128)}) %reduce-scatter.12.cloned.1.call-update) | async-done | bytes 2097168 | tf_op jit(solution)/shard_map/reduce_scatter | solution.py:286
  (320 shorter events, 291.4 us)
Async XLA Ops:
  7.2 163.4 %all-gather.10.cloned.1.call-start = ((), (), s32[]{:S(2)}) async-start(), calls=%async_computation.9 | async-start | bytes 2162688 | tf_op jit(solution)/shard_map/all_gather | solution.py:104
  8.8 164.4 %all-gather.12.cloned.1.call-start = ((), (), s32[]{:S(2)}) async-start(), calls=%async_computation.10 | async-start | bytes 2162688 | tf_op jit(solution)/shard_map/all_gather | solution.py:103
  9.5 167.9 %all-gather.14.cloned.1.call-start = ((), (), s32[]{:S(2)}) async-start(), calls=%async_computation.11 | async-start | bytes 2162688 | tf_op jit(solution)/shard_map/all_gather | solution.py:105
  10.3 253.0 %all-gather.18.cloned.1.call-start = ((), (), s32[]{:S(2)}) async-start(), calls=%async_computation.13 | async-start | bytes 34603008 | tf_op jit(solution)/shard_map/all_gather | solution.py:148
  10.9 312.6 %all-reduce.34.cloned.1.call-start = ((), (), s32[]{:S(2)}) async-start(), calls=%async_computation.32 | async-start | bytes 2097152 | tf_op jit(solution)/shard_map/psum | solution.py:29
  277.8 102.2 %all-gather.16.cloned.1.call-start = ((), (), s32[]{:S(2)}) async-start(), calls=%async_computation.12 | async-start | bytes 8650752 | tf_op jit(solution)/shard_map/all_gather | solution.py:142
  325.3 106.0 %all-gather.20.cloned.1.call-start = ((), (), s32[]{:S(2)}) async-start(), calls=%async_computation.14 | async-start | bytes 6488064 | tf_op jit(solution)/shard_map/all_gather | solution.py:157
  326.0 150.5 %all-gather.22.cloned.1.call-start = ((), (), s32[]{:S(2)}) async-start(), calls=%async_computation.15 | async-start | bytes 2162688 | tf_op jit(solution)/shard_map/all_gather | solution.py:159
  326.8 198.7 %all-reduce.24.cloned.1.call-start = ((), (), s32[]{:S(2)}) async-start(), calls=%async_computation.16 | async-start | bytes 2097152 | tf_op jit(solution)/shard_map/psum | solution.py:29
  480.0 101.0 %all-gather.24.cloned.1.call-start = ((), (), s32[]{:S(2)}) async-start(), calls=%async_computation.17 | async-start | bytes 8650752 | tf_op jit(solution)/shard_map/all_gather | solution.py:161
  480.5 155.2 %all-gather.26.cloned.1.call-start = ((), (), s32[]{:S(2)}) async-start(), calls=%async_computation.18 | async-start | bytes 8650752 | tf_op jit(solution)/shard_map/all_gather | solution.py:163
  481.3 227.5 %all-reduce.26.cloned.1.call-start = ((), (), s32[]{:S(2)}) async-start(), calls=%async_computation.19 | async-start | bytes 2097152 | tf_op jit(solution)/shard_map/psum | solution.py:29
  665.1 130.5 %all-reduce.28.cloned.1.call-start = ((), (), s32[]{:S(2)}) async-start(), calls=%async_computation.20 | async-start | bytes 2097152 | tf_op jit(solution)/shard_map/psum | solution.py:29
  750.3 176.5 %reduce-scatter.14.cloned.1.call-start = ((), (), s32[]{:S(2)}) async-start(), calls=%async_computation.22 | async-start | bytes 17301504 | tf_op jit(solution)/shard_map/reduce_scatter | solution.py:288
  811.0 176.6 %all-reduce.32.cloned.1.call-start = ((), (), s32[]{:S(2)}) async-start(), calls=%async_computation.31 | async-start | bytes 3145728 | tf_op jit(solution)/shard_map/psum | solution.py:29
  937.1 311.3 %all-reduce.30.cloned.1.call-start = ((), (), s32[]{:S(2)}) async-start(), calls=%async_computation.30 | async-start | bytes 8388608
  949.6 300.4 %reduce-scatter.28.cloned.1.call-start = ((), (), s32[]{:S(2)}) async-start(), calls=%async_computation.29 | async-start | bytes 1081344
  996.0 272.3 %reduce-scatter.22.cloned.1.call-start = ((), (), s32[]{:S(2)}) async-start(), calls=%async_computation.26 | async-start | bytes 4325376 | tf_op jit(solution)/shard_map/reduce_scatter | solution.py:357
  1000.0 376.4 %reduce-scatter.20.cloned.1.call-start = ((), (), s32[]{:S(2)}) async-start(), calls=%async_computation.25 | async-start | bytes 12976128 | tf_op jit(solution)/shard_map/reduce_scatter | solution.py:355
  1007.8 488.0 %reduce-scatter.26.cloned.1.call-start = ((), (), s32[]{:S(2)}) async-start(), calls=%async_computation.28 | async-start | bytes 17301504 | tf_op jit(solution)/shard_map/reduce_scatter | solution.py:361
  1017.1 598.2 %reduce-scatter.24.cloned.1.call-start = ((), (), s32[]{:S(2)}) async-start(), calls=%async_computation.27 | async-start | bytes 17301504 | tf_op jit(solution)/shard_map/reduce_scatter | solution.py:359
  1026.5 674.7 %reduce-scatter.18.cloned.1.call-start = ((), (), s32[]{:S(2)}) async-start(), calls=%async_computation.24 | async-start | bytes 4325376 | tf_op jit(solution)/shard_map/reduce_scatter | solution.py:351
  1030.2 756.4 %reduce-scatter.16.cloned.1.call-start = ((), (), s32[]{:S(2)}) async-start(), calls=%async_computation.23 | async-start | bytes 4325376 | tf_op jit(solution)/shard_map/reduce_scatter | solution.py:349
  1033.1 1050.9 %reduce-scatter.12.cloned.1.call-start = ((), (), s32[]{:S(2)}) async-start(), calls=%async_computation.21 | async-start | bytes 69206016 | tf_op jit(solution)/shard_map/reduce_scatter | solution.py:286
  (65 other events, 2673.1 us)
Sparse Core Ops, SparseCore 0:
  11.0 46.2 all-gather.9
  59.5 42.8 all-gather.11
  104.7 42.9 all-gather.13
  149.8 113.4 all-gather.17
  277.9 45.5 all-reduce.33
  326.4 53.5 all-gather.15
  382.6 48.6 all-gather.19
  433.8 42.6 all-gather.21
  480.1 45.3 all-reduce.23
  527.6 53.3 all-gather.23
  583.3 52.3 all-gather.25
  665.2 43.5 all-reduce.25
  750.4 45.1 all-reduce.27
  811.1 115.6 reduce-scatter.13
  937.2 50.3 all-reduce.31
  990.8 111.3 all-reduce.29
  1105.5 77.0 reduce-scatter.27
  1187.1 81.2 reduce-scatter.21
  1272.8 103.6 reduce-scatter.19
  1381.3 114.4 reduce-scatter.25
  1500.7 114.4 reduce-scatter.23
  1619.9 81.2 reduce-scatter.17
  1705.4 81.1 reduce-scatter.15
  1791.6 292.3 reduce-scatter.11
where the time goes:
time: 2100 us; the launch traced here: 2090 us
  waiting for transfers between devices  1440 us (69%)
  blocking collectives  340 us (16%)
  matrix products  121 us (6%)
  local copies, waits for them, and re-layouts  106 us (5%)
  other arithmetic  64 us (3%)
    reduce_scatter x1, waiting for transfers between devices, shards(): lax.psum_scatter(summed[:span_rows], 'dp', scatter_dimension=0, tiled=True)  297 us
    unnamed x2, blocking collectives  258 us
    psum x5, waiting for transfers between devices, head_total(): return lax.psum(partial_sum, 'grp')  214 us
    reduce_scatter x1, waiting for transfers between devices, shards(): lax.psum_scatter(grad_up, 'dp', scatter_dimension=0, tiled=True)  120 us
    reduce_scatter x1, waiting for transfers between devices, shards(): lax.psum_scatter(grad_down, 'dp', scatter_dimension=1, tiled=True)  119 us
    reduce_scatter x1, waiting for transfers between devices, shards(): lax.psum_scatter(grad_attn_weight, 'dp', scatter_dimension=0, tiled=True)  108 us
    reduce_scatter x1, waiting for transfers between devices, shards(): lax.psum_scatter(image_term(slot_image_pair, grad_image, pair_count * lax...  107 us
    reduce_scatter x1, waiting for transfers between devices, shards(): lax.psum_scatter(grad_mixer, 'dp', scatter_dimension=1, tiled=True)  85.9 us
  transfers between devices with their start and end apart: 24, of which 19 were waited for; matrix products, arithmetic and copies ran while one was open for 9% of the time, Pallas kernels for 0%

commit v1 on v0

v1 whole, which is shorter than its diff:
```python
from functools import partial

import jax
import jax.numpy as jnp
from jax import lax
from jax.sharding import PartitionSpec as P

HD = 64
RHD = 128
NL = 64
EPSILON = 1e-05
NEG_FILL = -1e30
GRP = 4
XS = 4
YS = 4
CS = 2
DP = XS * YS * CS
BF = jnp.bfloat16
F32 = jnp.float32


def dot(left, right, left_dims, right_dims):
    return lax.dot_general(
        left, right, (((left_dims,), (right_dims,)), ((), ())), preferred_element_type=F32
    )


def fetch(values, step_x, step_y, step_core):
    pairs = []
    for x in range(XS):
        for y in range(YS):
            for core in range(CS):
                source = (((x + step_x) % XS) * YS + (y + step_y) % YS) * CS + (core ^ step_core)
                pairs.append((source, (x * YS + y) * CS + core))
    return lax.ppermute(values, "dp", pairs)


def coordinates():
    place = lax.axis_index("dp")
    return place // (YS * CS), place // CS % YS, place % CS


def ring(values, axis):
    steps = [(step, 0) if axis == 0 else (0, step) for step in range(4)]
    return [values] + [fetch(values, *step, 0) for step in steps[1:]]


def gather_offsets(values):
    over_y = jnp.stack(ring(values, 1))
    over_x = jnp.stack(ring(over_y, 0))
    return jnp.stack([over_x, fetch(over_x, 0, 0, 1)])


def gather_small(values):
    x, y, core = coordinates()
    rows = gather_offsets(values)
    rows = jnp.roll(rows, (core, x, y), axis=(0, 1, 2))
    rows = jnp.moveaxis(rows, 0, 2)
    return rows.reshape((DP,) + values.shape)


def dp_total(values):
    values = values + fetch(values, 0, 0, 1)
    for axis in (0, 1):
        parts = ring(values, axis)
        values = (parts[0] + parts[2]) + (parts[1] + parts[3])
    return values


def scatter_offsets(values):
    values = values[0] + fetch(values[1], 0, 0, 1)
    values = values[0] + sum(fetch(values[step], -step, 0, 0) for step in range(1, XS))
    return values[0] + sum(fetch(values[step], 0, -step, 0) for step in range(1, YS))


def grp_gather(values):
    spread = jnp.broadcast_to(values[None], (GRP,) + values.shape)
    return lax.all_to_all(spread, "grp", 0, 0)


def grp_scatter(values, sent):
    rows = values.shape[0] // GRP
    blocks = values.astype(sent).reshape(GRP, rows, values.shape[1])
    return lax.all_to_all(blocks, "grp", 0, 0).astype(F32)


def total(parts):
    return (parts[0] + parts[1]) + (parts[2] + parts[3])


def row_norm(values):
    center = values - jnp.mean(values, axis=-1, keepdims=True)
    spread = jnp.mean(center * center, axis=-1, keepdims=True)
    scale_rows = lax.rsqrt(spread + EPSILON)
    return center * scale_rows, scale_rows


def row_norm_back(grad_normed, normed, scale_rows, scale_gain):
    grad_hat = grad_normed * scale_gain
    return scale_rows * (
        grad_hat
        - jnp.mean(grad_hat, axis=-1, keepdims=True)
        - normed * jnp.mean(grad_hat * normed, axis=-1, keepdims=True)
    )


def shards(
    caption_token_index,
    lengths,
    slot_image_pair,
    features,
    text_table,
    latents,
    sampler_gain,
    sampler_query,
    sampler_source,
    sampler_mixer,
    norm_gain_one,
    attention_in,
    norm_gain_two,
    attention_out,
    norm_gain_three,
    feed_up,
    norm_gain_four,
    feed_down,
    cotangent,
):
    group = lax.axis_index("grp")
    place = lax.axis_index("dp")
    width = feed_down.shape[1] * DP
    hidden = feed_down.shape[0] * GRP
    own = width // DP
    local = attention_out.shape[0]
    local_ff = feed_up.shape[1]
    patches, feature_width = features.shape[1:]
    tokens = cotangent.shape[1]
    spans = caption_token_index.shape[1]
    own_rows = tokens // GRP

    quarter = patches // GRP
    feature_part = lax.dynamic_slice_in_dim(features[0], group * quarter, quarter, 0)
    source_part = sampler_source.reshape(own, local)
    first_part = jnp.concatenate(
        [sampler_mixer.T, source_part, feature_part, attention_out.T, attention_in.reshape(own, 3 * local)],
        axis=1,
    )
    second_part = jnp.concatenate([feed_up, feed_down.T], axis=1)
    first_all = lax.all_gather(first_part, "dp", axis=0, tiled=True)
    second_all = lax.all_gather(second_part, "dp", axis=0, tiled=True)
    mixer_t = first_all[:, :local]
    source_weight = first_all[:, local : 2 * local].reshape(feature_width, 2 * local)
    feature_all = first_all[:, 2 * local : 2 * local + feature_width].reshape(DP, quarter, feature_width)
    out_t = first_all[:, 2 * local + feature_width : 3 * local + feature_width]
    in_weight = first_all[:, 3 * local + feature_width :]
    up_weight = second_all[:, :local_ff]
    down_t = second_all[:, local_ff:]

    flat_ids = caption_token_index[0]
    gain_two_pad = jnp.pad(norm_gain_two, (0, own - norm_gain_two.shape[0]))
    small = jnp.stack(
        [
            sampler_gain,
            norm_gain_one,
            norm_gain_three,
            norm_gain_four,
            gain_two_pad,
            (flat_ids // 256).astype(BF),
            (flat_ids % 256).astype(BF),
        ],
        axis=0,
    )
    small = jnp.concatenate([latents.T, small, jnp.zeros((9, own), BF)], axis=0)
    smalls = gather_small(small)
    latent_values = jnp.moveaxis(smalls[:, :own].reshape(width, NL), 1, 0).astype(F32)
    gains = smalls[:, own:].astype(F32)
    query_gain, gain_one, gain_three = (gains[:, i].reshape(width) for i in range(3))
    gain_four = gains[:, 3].reshape(local_ff)
    gain_two = gains[:, 4, : norm_gain_two.shape[0]].reshape(local)
    all_ids = (gains[:, 5] * 256 + gains[:, 6]).astype(jnp.int32)

    latent_hat, latent_scale = row_norm(latent_values)
    query_input = (latent_hat * query_gain).astype(BF)
    query_own = lax.dynamic_slice_in_dim(query_input, place * own, own, 1)
    latent_hat_own = lax.dynamic_slice_in_dim(latent_hat, place * own, own, 1)
    gain_row = jnp.broadcast_to(sampler_gain[None], (8, own))
    query_sums = dp_total(dot(jnp.concatenate([query_own, gain_row], axis=0), sampler_query, 1, 0))
    query_rows = query_sums[:NL]
    gain_rows = query_sums[NL : NL + 1]
    sampler_heads = local // RHD
    query_heads = query_rows.astype(BF).reshape(NL, sampler_heads, RHD)

    table_rows = text_table.shape[0]
    table_block = lax.all_to_all(text_table, "grp", 1, 0, tiled=True)
    x, y, core = coordinates()
    by_offset = jnp.roll(
        jnp.moveaxis(all_ids.reshape(XS, YS, CS, spans), 2, 0), (-core, -x, -y), axis=(0, 1, 2)
    )

    def block_rows(ids):
        span = table_rows * DP
        held = ids % span // table_rows == place
        return jnp.where(held, ids // span * table_rows + ids % table_rows, -1)

    def one_hot(ids):
        return (block_rows(ids)[:, None] == jnp.arange(GRP * table_rows, dtype=jnp.int32)[None]).astype(BF)

    picked = dot(one_hot(by_offset.reshape(-1)), table_block, 1, 0).astype(BF)
    text_cols = scatter_offsets(picked.reshape(CS, XS, YS, spans, local))
    text_rows = jnp.moveaxis(grp_gather(text_cols), 0, 1).reshape(spans, width)

    pair_part = lax.dynamic_index_in_dim(feature_all, slot_image_pair[0], 0, keepdims=False)
    pair_rows = grp_gather(pair_part).reshape(patches, feature_width)
    sources = dot(pair_rows, source_weight, 1, 0).astype(BF)
    key_heads = sources[:, :local].reshape(patches, sampler_heads, RHD)
    value_heads = sources[:, local:].reshape(patches, sampler_heads, RHD)
    sampler_factor = RHD ** (-0.5)
    scores = (
        jnp.einsum("lhe,nhe->hln", query_heads, key_heads, preferred_element_type=F32) * sampler_factor
    )
    exponent = jnp.exp(scores - jnp.max(scores, axis=-1, keepdims=True))
    sampler_prob = exponent / jnp.sum(exponent, axis=-1, keepdims=True)
    sampler_low = sampler_prob.astype(BF)
    sampled = jnp.einsum("hln,nhe->lhe", sampler_low, value_heads, preferred_element_type=F32)
    sampled = sampled.reshape(NL, local).astype(BF)
    mixed = total(grp_scatter(dot(sampled, mixer_t, 1, 1), F32))
    latent_rows = lax.dynamic_slice_in_dim(latent_values, group * (NL // GRP), NL // GRP, 0)
    image_rows = grp_gather((latent_rows + mixed).astype(BF)).reshape(NL, width)

    inputs = jnp.concatenate([image_rows, text_rows], axis=0).astype(F32)
    first_hat, first_scale = row_norm(inputs)
    first_input = (first_hat * gain_one).astype(BF)

    def own_of(values):
        return lax.dynamic_slice_in_dim(values, group * own_rows, own_rows, 0)

    projected = dot(first_input, in_weight, 1, 0).astype(BF)
    heads_here = local // HD
    query_text, key_text, value_text = (
        projected[:, i * local : (i + 1) * local].reshape(tokens, heads_here, HD) for i in range(3)
    )
    positions = jnp.arange(tokens, dtype=jnp.int32)
    allowed = (positions[None, :] <= positions[:, None]) & (positions[None, :] < NL + lengths[0])
    text_factor = HD ** (-0.5)
    scores = jnp.einsum("qhe,khe->hqk", query_text, key_text, preferred_element_type=F32) * text_factor
    scores = jnp.where(allowed[None], scores, NEG_FILL)
    exponent = jnp.exp(scores - jnp.max(scores, axis=-1, keepdims=True))
    probability = exponent / jnp.sum(exponent, axis=-1, keepdims=True)
    weights_low = probability.astype(BF)
    attended = jnp.einsum("hqk,khe->qhe", weights_low, value_text, preferred_element_type=F32)
    attended = attended.reshape(tokens, local)

    second_mean = jnp.mean(attended, axis=-1, keepdims=True)
    second_center = attended - second_mean
    second_square = jnp.sum(second_center * second_center, axis=-1, keepdims=True)
    second_sums = grp_gather(jnp.concatenate([second_mean, second_square], axis=1))
    branch_part = dot((second_center * gain_two).astype(BF), out_t, 1, 1)
    branch_parts = grp_scatter(branch_part, BF)
    gain_out = grp_gather(dot(jnp.broadcast_to(gain_two.astype(BF)[None], (8, local)), out_t, 1, 1)[:1])
    second_means = second_sums[:, :, :1]
    second_all = jnp.mean(second_means, axis=0)
    second_spread = (
        jnp.sum(second_sums[:, :, 1:] + local * jnp.square(second_means - second_all), axis=0) / width
    )
    second_scale = lax.rsqrt(second_spread + EPSILON)
    second_hat = (attended - second_all) * second_scale
    second_input = (second_hat * gain_two).astype(BF)
    shift_own = lax.dynamic_slice_in_dim(second_means - second_all, group * own_rows, own_rows, 1)
    branch = own_of(second_scale) * total(branch_parts + shift_own * gain_out)
    gain_out_total = total(gain_out)

    middle = own_of(inputs) + branch
    third_hat, third_scale = row_norm(middle)
    third_input = grp_gather((third_hat * gain_three).astype(BF)).reshape(tokens, width)
    up_rows = dot(third_input, up_weight, 1, 0)
    activated, gelu_back = jax.vjp(partial(jax.nn.gelu, approximate=False), up_rows)
    grad_output = cotangent[0]
    grad_fourth = dot(grad_output, down_t, 1, 0)
    grad_hat = grad_fourth * gain_four
    fourth_mean = jnp.mean(activated, axis=-1, keepdims=True)
    fourth_center = activated - fourth_mean
    fourth_sums = grp_gather(
        jnp.concatenate(
            [
                fourth_mean,
                jnp.sum(fourth_center * fourth_center, axis=-1, keepdims=True),
                jnp.sum(grad_hat, axis=-1, keepdims=True),
                jnp.sum(grad_hat * fourth_center, axis=-1, keepdims=True),
            ],
            axis=1,
        )
    )
    fourth_means = fourth_sums[:, :, :1]
    fourth_all = jnp.mean(fourth_means, axis=0)
    fourth_shift = fourth_means - fourth_all
    fourth_scale = lax.rsqrt(
        jnp.sum(fourth_sums[:, :, 1:2] + local_ff * fourth_shift * fourth_shift, axis=0) / hidden + EPSILON
    )
    fourth_hat = (activated - fourth_all) * fourth_scale
    fourth_input = (fourth_hat * gain_four).astype(BF)
    sum_grad = total(fourth_sums[:, :, 2:3]) / hidden
    sum_cross = (
        fourth_scale * total(fourth_sums[:, :, 3:] + fourth_shift * fourth_sums[:, :, 2:3]) / hidden
    )
    grad_active = fourth_scale * (grad_hat - sum_grad - fourth_hat * sum_cross)
    grad_up_rows = gelu_back(grad_active)[0].astype(BF)
    grad_gain_four = jnp.sum(grad_fourth * fourth_hat, axis=0)
    grad_third = total(grp_scatter(dot(grad_up_rows, up_weight, 1, 1), BF))

    result = middle + total(grp_scatter(dot(fourth_input, down_t, 1, 1), BF))
    layer_output = grp_gather(result).reshape(1, tokens, width)

    ff_grads = jnp.concatenate(
        [
            dot(third_input, grad_up_rows, 0, 0).astype(BF),
            dot(grad_output, fourth_input, 0, 0).astype(BF),
        ],
        axis=1,
    )
    ff_grads = lax.psum_scatter(ff_grads, "dp", scatter_dimension=0, tiled=True)

    grad_middle = own_of(grad_output).astype(F32) + row_norm_back(
        grad_third, third_hat, third_scale, gain_three
    )
    grad_gain_three = jnp.sum(grad_third * third_hat, axis=0)
    branch_low = grad_middle.astype(BF)
    branch_wide = branch_low.astype(F32)
    second_back = jnp.concatenate(
        [
            jnp.sum(branch_wide * gain_out_total, axis=-1, keepdims=True),
            jnp.sum(branch_wide * branch, axis=-1, keepdims=True),
        ],
        axis=1,
    )
    grad_branch = grp_gather(branch_low).reshape(tokens, width)
    second_back = grp_gather(second_back).reshape(tokens, 2) / width
    grad_gain_three = total(grp_gather(grad_gain_three))

    grad_second = dot(grad_branch, out_t, 1, 0)
    grad_attended = second_scale * (
        grad_second * gain_two - second_back[:, :1] - second_hat * second_back[:, 1:]
    )
    grad_gain_two = jnp.sum(grad_second * second_hat, axis=0)
    grad_att = grad_attended.astype(BF).reshape(tokens, heads_here, HD)
    grad_value = jnp.einsum("hqk,qhe->khe", weights_low, grad_att, preferred_element_type=F32)
    grad_weights = jnp.einsum("qhe,khe->hqk", grad_att, value_text, preferred_element_type=F32)
    grad_scores = probability * (
        grad_weights - jnp.sum(probability * grad_weights, axis=-1, keepdims=True)
    )
    grad_scores = grad_scores.astype(BF)
    grad_query = (
        jnp.einsum("hqk,khe->qhe", grad_scores, key_text, preferred_element_type=F32) * text_factor
    )
    grad_key = (
        jnp.einsum("hqk,qhe->khe", grad_scores, query_text, preferred_element_type=F32) * text_factor
    )
    grad_projected = jnp.concatenate(
        [part.reshape(tokens, local) for part in (grad_query, grad_key, grad_value)], axis=1
    ).astype(BF)
    grad_first = total(grp_scatter(dot(grad_projected, in_weight, 1, 1), BF))
    first_hat_own = own_of(first_hat)
    input_own = grad_middle + row_norm_back(grad_first, first_hat_own, own_of(first_scale), gain_one)
    grad_gain_one = total(grp_gather(jnp.sum(grad_first * first_hat_own, axis=0)))
    input_low = grp_gather(input_own.astype(BF)).reshape(tokens, width)
    input_grad = grp_gather(input_own).reshape(1, tokens, width)

    text_low = lax.dynamic_slice_in_dim(input_low[NL:], group * local, local, 1)
    text_all = gather_offsets(text_low).reshape(DP * spans, local)
    table_sums = dot(one_hot(by_offset.reshape(-1)), text_all, 0, 0).astype(BF)
    table_sums = lax.all_to_all(table_sums, "grp", 0, 1, tiled=True)
    table_grad = table_sums.astype(F32)

    image_low = input_low[:NL]
    grad_sampled = dot(image_low, mixer_t, 1, 0).astype(BF).reshape(NL, sampler_heads, RHD)
    grad_source_value = jnp.einsum("hln,lhe->nhe", sampler_low, grad_sampled, preferred_element_type=F32)
    grad_sampler = jnp.einsum("lhe,nhe->hln", grad_sampled, value_heads, preferred_element_type=F32)
    grad_sampler = sampler_prob * (
        grad_sampler - jnp.sum(sampler_prob * grad_sampler, axis=-1, keepdims=True)
    )
    grad_sampler = grad_sampler.astype(BF)
    grad_query_heads = (
        jnp.einsum("hln,nhe->lhe", grad_sampler, key_heads, preferred_element_type=F32) * sampler_factor
    )
    grad_source_key = (
        jnp.einsum("hln,lhe->nhe", grad_sampler, query_heads, preferred_element_type=F32) * sampler_factor
    )
    grad_sources = jnp.concatenate(
        [grad_source_key.reshape(patches, local), grad_source_value.reshape(patches, local)], axis=1
    ).astype(BF)
    grad_query_total = dp_total(grad_query_heads.reshape(NL, local))
    grad_query_low = grad_query_total.astype(BF)
    grad_query_wide = grad_query_low.astype(F32)
    sampler_query_grad = dot(query_own, grad_query_low, 0, 0)
    sampler_back = jnp.concatenate(
        [
            dot(grad_query_low, sampler_query, 1, 1),
            jnp.sum(grad_query_wide * gain_rows, axis=-1, keepdims=True),
            jnp.sum(grad_query_wide * query_rows, axis=-1, keepdims=True),
        ],
        axis=1,
    )
    sampler_back = total(grp_gather(sampler_back))
    grad_query_norm = sampler_back[:, :own]
    sampler_means = sampler_back[:, own:] / width
    grad_latent_norm = latent_scale * (
        grad_query_norm * sampler_gain.astype(F32)
        - sampler_means[:, :1]
        - latent_hat_own * sampler_means[:, 1:]
    )
    sampler_gain_grad = jnp.sum(grad_query_norm * latent_hat_own, axis=0)

    mixer_and_latents = dot(
        image_low, jnp.concatenate([sampled, jnp.eye(NL, dtype=BF)], axis=1), 0, 0
    ).astype(BF)
    per_own = norm_gain_two.shape[0]
    gain_two_cols = jnp.pad(grad_gain_two.reshape(DP, per_own), ((0, 0), (0, own - per_own)))
    gain_cols = jnp.stack(
        [grad_gain_one, grad_gain_three, grad_gain_four, gain_two_cols.reshape(-1)], axis=1
    ).astype(BF)
    rest = jnp.concatenate(
        [
            dot(first_input, grad_projected, 0, 0).astype(BF),
            dot(grad_branch, second_input, 0, 0).astype(BF),
            dot(pair_rows, grad_sources, 0, 0).astype(BF).reshape(width, local),
            mixer_and_latents,
            gain_cols,
        ],
        axis=1,
    )
    rest = lax.psum_scatter(rest, "dp", scatter_dimension=0, tiled=True).astype(F32)
    cut = 3 * local
    attention_in_grad = rest[:, :cut].reshape(own, 3, local)
    attention_out_grad = rest[:, cut : cut + local].T
    sampler_source_grad = rest[:, cut + local : cut + 2 * local].reshape(own // 2, 2, local)
    sampler_mixer_grad = rest[:, cut + 2 * local : cut + 3 * local].T
    latents_grad = rest[:, cut + 3 * local : cut + 3 * local + NL].T + grad_latent_norm
    gain_grads = rest[:, cut + 3 * local + NL :]
    ff_grads = ff_grads.astype(F32)
    return (
        layer_output,
        input_grad,
        table_grad,
        latents_grad,
        sampler_gain_grad,
        sampler_query_grad,
        sampler_source_grad,
        sampler_mixer_grad,
        gain_grads[:, 0],
        attention_in_grad,
        gain_grads[:per_own, 3],
        attention_out_grad,
        gain_grads[:, 1],
        ff_grads[:, :local_ff],
        gain_grads[:, 2],
        ff_grads[:, local_ff:].T,
    )


def solution(mesh):
    return jax.shard_map(
        shards,
        mesh=mesh,
        in_specs=(
            P("dp", None),
            P("dp"),
            P("dp"),
            P("dp", None, None),
            P(("grp", "dp"), None),
            P(None, "dp"),
            P("dp"),
            P("dp", "grp"),
            P("dp", None, "grp"),
            P("grp", "dp"),
            P("dp"),
            P("dp", None, "grp"),
            P(("grp", "dp")),
            P("grp", "dp"),
            P("dp"),
            P("dp", "grp"),
            P(("grp", "dp")),
            P("grp", "dp"),
            P("dp", None, None),
        ),
        out_specs=(
            P("dp", None, None),
            P("dp", None, None),
            P(("grp", "dp"), None),
            P(None, "dp"),
            P("dp"),
            P("dp", "grp"),
            P("dp", None, "grp"),
            P("grp", "dp"),
            P("dp"),
            P("dp", None, "grp"),
            P(("grp", "dp")),
            P("grp", "dp"),
            P("dp"),
            P("dp", "grp"),
            P(("grp", "dp")),
            P("grp", "dp"),
        ),
        check_vma=False,
    )
```

time: 2100 us -> 715 us (0.34)
  waiting for transfers between devices: 1440 us -> 237 us
  blocking collectives: 340 us -> 0 us
  starting transfers between devices: 1.4 us -> 134 us
  local copies, waits for them, and re-layouts: 106 us -> 173 us
  matrix products: 121 us -> 90.3 us
    reduce_scatter x8 -> x0, waiting for transfers between devices: 940 us -> none  [the longest x1 297 us: shards(): lax.psum_scatter(summed[:span_rows], 'dp', scatter_dimension=0, tiled=True)]
    all_gather x9 -> x2, waiting for transfers between devices: 280 us -> 0.02 us  [the longest x1 0.02 us: shards(): second_all = lax.all_gather(second_part, 'dp', axis=0, tiled=True)]
    unnamed x2 -> x0, blocking collectives: 258 us -> none
    psum x5 -> x0, waiting for transfers between devices: 214 us -> none  [head_total(): return lax.psum(partial_sum, 'grp')]
    unnamed x26 -> x6, waiting for transfers between devices: 4.79 us -> 99.9 us
    all_to_all x0 -> x22, waiting for transfers between devices: none -> 87.9 us  [the longest x15 50.6 us: grp_gather(): return lax.all_to_all(spread, 'grp', 0, 0)]
    all_to_all x0 -> x22, starting transfers between devices: none -> 84.4 us  [the longest x15 55.4 us: grp_gather(): return lax.all_to_all(spread, 'grp', 0, 0)]
    psum x6 -> x0, blocking collectives: 59.6 us -> none  [row_total(): return lax.psum(partial_rows, 'grp')]
  transfers between devices with their start and end apart: 24 -> 61, of which waited for: 19 -> 41; matrix products, arithmetic and copies ran while one was open for 9% -> 22% of each run, Pallas kernels for 0% -> 0%
where the time goes in v1:
time: 715 us; the launch traced here: 701 us
  waiting for transfers between devices  237 us (33%)
  local copies, waits for them, and re-layouts  173 us (24%)
  starting transfers between devices  134 us (19%)
  matrix products  90.3 us (13%)
  other arithmetic  49.7 us (7%)
  between operations  17.1 us (2%)
    unnamed x6, waiting for transfers between devices  99.9 us
    dot_general x23, matrix products, dot(): lax.dot_general(left, right, (((left_dims,), (right_dims,)), ((), ())), p...  78 us
    unnamed x159, local copies, waits for them, and re-layouts  67.2 us
    all_to_all x15, starting transfers between devices, grp_gather(): return lax.all_to_all(spread, 'grp', 0, 0)  55.4 us
    concatenate x1, local copies, waits for them, and re-layouts, shards(): jnp.concatenate([dot(first_input, grad_projected, 0, 0).astype(BF), dot(g...  52.5 us
    all_to_all x15, waiting for transfers between devices, grp_gather(): return lax.all_to_all(spread, 'grp', 0, 0)  50.6 us
    ppermute x35, waiting for transfers between devices, fetch(): return lax.ppermute(values, 'dp', pairs)  49.3 us
    ppermute x35, starting transfers between devices, fetch(): return lax.ppermute(values, 'dp', pairs)  49.1 us
  transfers between devices with their start and end apart: 61, of which 41 were waited for; matrix products, arithmetic and copies ran while one was open for 22% of the time, Pallas kernels for 0%

profile of v1, /device:TPU:0, one launch (start us, length us, event | category | flops | bytes accessed | tf_op | source)
XLA Modules:
  0.0 700.7 jit_solution(17053830083918414540)
XLA Ops:
  41.5 5.4 all-to-all-start.3
  55.9 6.8 all-to-all-done.3
  127.4 4.9 all-to-all-start.4
  147.7 5.5 all-to-all-done.1
  167.7 5.6 all-to-all-done.2
  193.6 7.3 %all-to-all-done.6 = bf16[4,32,2048]{2,1,0:T(8,128)(2,1)S(1)} async-done(((bf16[4,32,2048]{2,1,0:T(8,128)(2,1)}), bf16[4,32,2048]{2,1,0:T(8,128)(2,1)S(1)}, u32[]{:S(2)}, u32[]{:S(2)}) %all-to-all-start.6) | async-done | bytes 524320 | tf_op jit(solution)/shard_map/all_to_all | solution.py:84
  207.8 7.4 %all-to-all-done.8 = bf16[4,32,2048]{2,1,0:T(8,128)(2,1)S(1)} async-done(((bf16[4,32,2048]{2,1,0:T(8,128)(2,1)}), bf16[4,32,2048]{2,1,0:T(8,128)(2,1)S(1)}, u32[]{:S(2)}, u32[]{:S(2)}) %all-to-all-start.8) | async-done | bytes 524320 | tf_op jit(solution)/shard_map/all_to_all | solution.py:78
  215.2 8.1 %fusion.191 = (f32[128]{0:T(128)S(1)}, f32[128,2048]{1,0:T(8,128)S(1)}, f32[128,2048]{1,0:T(8,128)}, f32[128,2048]{1,0:T(8,128)}) fusion(bf16[128,2048]{1,0:T(8,128)(2,1)S(1)} %bitcast.363, bf16[2048,4096]{1,0:T(8,128)(2,1)} %all-gather.5.cloned.1.call-done), kind=kOutput, calls=%fused_computation.398 | convolution fusion | flops 1090781056 | bytes 12059136 | tf_op jit(solution)/shard_map/dot_general | solution.py:23
  240.1 7.3 %fusion.22 = bf16[128,2048]{1,0:T(8,128)(2,1)} fusion(bf16[128,2048]{1,0:T(8,128)(2,1)S(1)} %get-tuple-element.147, bf16[2048,4096]{1,0:T(8,128)(2,1)} %all-gather.5.cloned.1.call-done), kind=kOutput, calls=%fused_computation.27 | convolution fusion | flops 1074003968 | bytes 9437184 | tf_op jit(solution)/shard_map/dot_general | solution.py:23
  250.9 7.1 %fusion.25 = bf16[128,2048]{1,0:T(8,128)(2,1)} fusion(bf16[2048,4096]{1,0:T(8,128)(2,1)} %all-gather.5.cloned.1.call-done, f32[128,2048]{1,0:T(8,128)S(1)} %get-tuple-element.139, f32[128]{0:T(128)S(1)} %get-tuple-element.188, f32[128]{0:T(128)S(1)} %broadcast_multiply_fusion.5, f32[2048]{0:T(1024)S(1)} %mul.503), kind=kOutput, calls=%fused_computation.28 | convolution fusion | flops 1075052544 | bytes 9970688 | tf_op jit(solution)/shard_map/dot_general | solution.py:23
  269.7 5.0 all-to-all-done.10
  292.1 5.3 all-to-all-done.20
  303.2 7.4 %all-to-all-done.13 = bf16[4,32,2048]{2,1,0:T(8,128)(2,1)S(1)} async-done(((bf16[4,32,2048]{2,1,0:T(8,128)(2,1)}), bf16[4,32,2048]{2,1,0:T(8,128)(2,1)S(1)}, u32[]{:S(2)}, u32[]{:S(2)}) %all-to-all-start.13) | async-done | bytes 524320 | tf_op jit(solution)/shard_map/all_to_all | solution.py:78
  320.2 5.9 fusion.31
  335.7 5.5 convolution_convert_fusion
  357.4 7.4 %all-to-all-done.17 = bf16[4,32,2048]{2,1,0:T(8,128)(2,1)S(1)} async-done(((bf16[4,32,2048]{2,1,0:T(8,128)(2,1)}), bf16[4,32,2048]{2,1,0:T(8,128)(2,1)S(1)}, u32[]{:S(2)}, u32[]{:S(2)}) %all-to-all-start.17) | async-done | bytes 524320 | tf_op jit(solution)/shard_map/all_to_all | solution.py:78
  382.9 52.5 %concatenate.89 = bf16[2048,3140]{0,1:T(8,128)(2,1)} concatenate(bf16[2048,1536]{0,1:T(8,128)(2,1)} %convolution_convert_fusion, bf16[2048,512]{0,1:T(8,128)(2,1)} %convolution_convert_fusion.3, bf16[2048,512]{0,1:T(8,128)(2,1)} %copy.327, bf16[2048,576]{0,1:T(8,128)(2,1)S(1)} %convolution_convert_fusion.2, bf16[2048,1]{0,1:T(2,128)(2,1)} %convert_bitcast_fusion.3, ...), dimensions={1} | concatenate | bytes 25722880 | tf_op jit(solution)/shard_map/concatenate | solution.py:419
  435.4 16.9 %copy.343 = bf16[2048,3140]{1,0:T(8,128)(2,1)} copy(bf16[2048,3140]{0,1:T(8,128)(2,1)} %concatenate.89) | data formatting | bytes 25722880
  458.4 7.5 %pad_maximum_fusion = bf16[2048,4096]{0,1:T(8,128)(2,1)} fusion(bf16[2048,2048]{0,1:T(8,128)(2,1)S(1)} %convert_bitcast_fusion, bf16[2048,2048]{0,1:T(8,128)(2,1)S(1)} %convolution_convert_fusion.1), kind=kLoop, calls=%fused_computation.2 | loop fusion | flops 33554432 | bytes 33554432 | tf_op jit(solution)/shard_map/concatenate | solution.py:312
  466.0 22.1 %copy.345 = bf16[2048,4096]{1,0:T(8,128)(2,1)} copy(bf16[2048,4096]{0,1:T(8,128)(2,1)} %pad_maximum_fusion) | data formatting | bytes 33554432
  512.5 6.8 collective-permute-done.25
  552.0 5.4 fusion.44
  564.1 8.9 %all-to-all-done.18 = bf16[4,256,512]{2,1,0:T(8,128)(2,1)S(1)} async-done(((bf16[4,256,512]{2,1,0:T(8,128)(2,1)}), bf16[4,256,512]{2,1,0:T(8,128)(2,1)S(1)}, u32[]{:S(2)}, u32[]{:S(2)}) %all-to-all-start.18) | async-done | bytes 1048608 | tf_op jit(solution)/shard_map/all_to_all | solution.py:369
  583.0 99.9 %reduce-scatter.9.cloned.1.call-done = bf16[64,4096]{1,0:T(8,128)(2,1)} async-done(((bf16[2048,4096]{1,0:T(8,128)(2,1)}), bf16[64,4096]{1,0:T(8,128)(2,1)}) %reduce-scatter.9.cloned.1.call-update) | async-done | bytes 524304
  (482 shorter events, 361.5 us)
Async XLA Ops:
  7.2 101.8 %all-gather.3.cloned.1.call-start = ((), (), s32[]{:S(2)}) async-start(), calls=%async_computation.24 | async-start | bytes 17301504 | tf_op jit(solution)/shard_map/all_gather | solution.py:148
  12.5 195.3 %all-gather.5.cloned.1.call-start = ((), (), s32[]{:S(2)}) async-start(), calls=%async_computation.25 | async-start | bytes 17301504 | tf_op jit(solution)/shard_map/all_gather | solution.py:149
  41.5 21.2 %all-to-all-start.3 = ((bf16[256,4,512]{0,2,1:T(8,128)(2,1)}), bf16[256,4,512]{0,2,1:T(8,128)(2,1)S(1)}, u32[]{:S(2)}, u32[]{:S(2)}) async-start(bf16[256,4,512]{0,2,1:T(8,128)(2,1)} %bitcast.35), calls=%async_computation.3 | async-start | bytes 2097152 | tf_op jit(solution)/shard_map/all_to_all | solution.py:193
  74.2 16.6 %collective-permute-start.8 = (f32[72,512]{1,0:T(8,128)S(1)}, f32[72,512]{1,0:T(8,128)}, u32[]{:S(2)}, u32[]{:S(2)}) collective-permute-start(f32[72,512]{1,0:T(8,128)S(1)} %add.565), channel_id=1, source_target_pairs={{16,0},{17,1},{18,2},{19,3},{20,4},{21,5},{22,6},{23,7},{24,8},{25... | collective-permute-start | bytes 442376 | tf_op jit(solution)/shard_map/ppermute | solution.py:35
  77.7 20.1 %collective-permute-start.17 = (bf16[4,64,512]{2,1,0:T(8,128)(2,1)}, bf16[4,64,512]{2,1,0:T(8,128)(2,1)S(1)}, u32[]{:S(2)}, u32[]{:S(2)}) collective-permute-start(bf16[4,64,512]{2,1,0:T(8,128)(2,1)} %get-tuple-element.158), channel_id=1, source_target_pairs={{8,0},{9,1},{10,2},{11,3},{12,4},{13,5},{14,6},{15,7},{16,8},{17,9... | collective-permute-start | bytes 786440 | tf_op jit(solution)/shard_map/ppermute | solution.py:35
  78.7 22.3 %collective-permute-start.15 = (bf16[4,64,512]{2,1,0:T(8,128)(2,1)}, bf16[4,64,512]{2,1,0:T(8,128)(2,1)S(1)}, u32[]{:S(2)}, u32[]{:S(2)}) collective-permute-start(bf16[4,64,512]{2,1,0:T(8,128)(2,1)} %get-tuple-element.159), channel_id=1, source_target_pairs={{24,0},{25,1},{26,2},{27,3},{28,4},{29,5},{30,6},{31,7},{0,8},{1,9... | collective-permute-start | bytes 786440 | tf_op jit(solution)/shard_map/ppermute | solution.py:35
  82.6 22.2 %collective-permute-start.16 = (bf16[4,64,512]{2,1,0:T(8,128)(2,1)S(1)}, bf16[4,64,512]{2,1,0:T(8,128)(2,1)S(1)}, u32[]{:S(2)}, u32[]{:S(2)}) collective-permute-start(bf16[4,64,512]{2,1,0:T(8,128)(2,1)S(1)} %get-tuple-element.157), channel_id=1, source_target_pairs={{16,0},{17,1},{18,2},{19,3},{20,4},{21,5},{22,6},{23,7},{24,8},{25... | collective-permute-start | bytes 786440 | tf_op jit(solution)/shard_map/ppermute | solution.py:35
  91.9 24.6 %collective-permute-start.12 = (f32[72,512]{1,0:T(8,128)S(1)}, f32[72,512]{1,0:T(8,128)}, u32[]{:S(2)}, u32[]{:S(2)}) collective-permute-start(f32[72,512]{1,0:T(8,128)S(1)} %add_add_fusion.1), channel_id=1, source_target_pairs={{2,0},{3,1},{4,2},{5,3},{6,4},{7,5},{0,6},{1,7},{10,8},{11,9},{12,... | collective-permute-start | bytes 442376 | tf_op jit(solution)/shard_map/ppermute | solution.py:35
  93.6 25.2 %collective-permute-start.13 = (f32[72,512]{1,0:T(8,128)S(1)}, f32[72,512]{1,0:T(8,128)}, u32[]{:S(2)}, u32[]{:S(2)}) collective-permute-start(f32[72,512]{1,0:T(8,128)S(1)} %add_add_fusion.1), channel_id=1, source_target_pairs={{6,0},{7,1},{0,2},{1,3},{2,4},{3,5},{4,6},{5,7},{14,8},{15,9},{8,1... | collective-permute-start | bytes 442376 | tf_op jit(solution)/shard_map/ppermute | solution.py:35
  97.9 20.9 %collective-permute-start.11 = (f32[72,512]{1,0:T(8,128)S(1)}, f32[72,512]{1,0:T(8,128)}, u32[]{:S(2)}, u32[]{:S(2)}) collective-permute-start(f32[72,512]{1,0:T(8,128)S(1)} %add_add_fusion.1), channel_id=1, source_target_pairs={{4,0},{5,1},{6,2},{7,3},{0,4},{1,5},{2,6},{3,7},{12,8},{13,9},{14,... | collective-permute-start | bytes 442376 | tf_op jit(solution)/shard_map/ppermute | solution.py:35
  112.0 14.6 %all-to-all-start = ((bf16[4,64,1024]{2,1,0:T(8,128)(2,1)}), bf16[4,64,1024]{2,1,0:T(8,128)(2,1)}, u32[]{:S(2)}, u32[]{:S(2)}) async-start(bf16[4,64,1024]{2,1,0:T(8,128)(2,1)} %broadcast_in_dim.73), calls=%async_computation | async-start | bytes 1048576 | tf_op jit(solution)/shard_map/all_to_all | solution.py:78
  247.4 14.2 %all-to-all-start.12 = ((bf16[4,32,2048]{2,1,0:T(8,128)(2,1)}), bf16[4,32,2048]{2,1,0:T(8,128)(2,1)S(1)}, u32[]{:S(2)}, u32[]{:S(2)}) async-start(bf16[4,32,2048]{2,1,0:T(8,128)(2,1)} %bitcast.385), calls=%async_computation.12 | async-start | bytes 1048576 | tf_op jit(solution)/shard_map/all_to_all | solution.py:84
  326.0 15.2 %all-to-all-start.15 = ((bf16[4,32,2048]{2,1,0:T(8,128)(2,1)}), bf16[4,32,2048]{2,1,0:T(8,128)(2,1)S(1)}, u32[]{:S(2)}, u32[]{:S(2)}) async-start(bf16[4,32,2048]{2,1,0:T(8,128)(2,1)} %bitcast.384), calls=%async_computation.15 | async-start | bytes 1048576 | tf_op jit(solution)/shard_map/all_to_all | solution.py:84
  356.7 218.2 %reduce-scatter.7.cloned.1.call-start = ((), (), s32[]{:S(2)}) async-start(), calls=%async_computation.26 | async-start | bytes 13516800
  452.4 230.4 %reduce-scatter.9.cloned.1.call-start = ((), (), s32[]{:S(2)}) async-start(), calls=%async_computation.27 | async-start | bytes 17301504
  498.9 20.4 %collective-permute-start.25 = (bf16[4,64,512]{2,1,0:T(8,128)(2,1)S(1)}, bf16[4,64,512]{2,1,0:T(8,128)(2,1)S(1)}, u32[]{:S(2)}, u32[]{:S(2)}) collective-permute-start(bf16[4,64,512]{2,1,0:T(8,128)(2,1)S(1)} %get-tuple-element.172), channel_id=1, source_target_pairs={{16,0},{17,1},{18,2},{19,3},{20,4},{21,5},{22,6},{23,7},{24,8},{25... | collective-permute-start | bytes 786440 | tf_op jit(solution)/shard_map/ppermute | solution.py:35
  500.7 20.3 %collective-permute-start.24 = (bf16[4,64,512]{2,1,0:T(8,128)(2,1)S(1)}, bf16[4,64,512]{2,1,0:T(8,128)(2,1)S(1)}, u32[]{:S(2)}, u32[]{:S(2)}) collective-permute-start(bf16[4,64,512]{2,1,0:T(8,128)(2,1)S(1)} %get-tuple-element.172), channel_id=1, source_target_pairs={{8,0},{9,1},{10,2},{11,3},{12,4},{13,5},{14,6},{15,7},{16,8},{17,9... | collective-permute-start | bytes 786440 | tf_op jit(solution)/shard_map/ppermute | solution.py:35
  502.7 27.8 %all-to-all-start.11 = ((f32[4,32,2048]{2,1,0:T(8,128)}), f32[4,32,2048]{2,1,0:T(8,128)S(1)}, u32[]{:S(2)}, u32[]{:S(2)}) async-start(f32[4,32,2048]{2,1,0:T(8,128)} %broadcast_in_dim.89), calls=%async_computation.11 | async-start | bytes 2097152 | tf_op jit(solution)/shard_map/all_to_all | solution.py:78
  506.3 18.9 %collective-permute-start.30 = (f32[64,512]{1,0:T(8,128)S(1)}, f32[64,512]{1,0:T(8,128)S(1)}, u32[]{:S(2)}, u32[]{:S(2)}) collective-permute-start(f32[64,512]{1,0:T(8,128)S(1)} %fusion.182), channel_id=1, source_target_pairs={{8,0},{9,1},{10,2},{11,3},{12,4},{13,5},{14,6},{15,7},{16,8},{17,9... | collective-permute-start | bytes 393224 | tf_op jit(solution)/shard_map/ppermute | solution.py:35
  507.7 17.4 %collective-permute-start.31 = (f32[64,512]{1,0:T(8,128)S(1)}, f32[64,512]{1,0:T(8,128)S(1)}, u32[]{:S(2)}, u32[]{:S(2)}) collective-permute-start(f32[64,512]{1,0:T(8,128)S(1)} %fusion.182), channel_id=1, source_target_pairs={{24,0},{25,1},{26,2},{27,3},{28,4},{29,5},{30,6},{31,7},{0,8},{1,9... | collective-permute-start | bytes 393224 | tf_op jit(solution)/shard_map/ppermute | solution.py:35
  509.4 18.3 %collective-permute-start.29 = (f32[64,512]{1,0:T(8,128)S(1)}, f32[64,512]{1,0:T(8,128)S(1)}, u32[]{:S(2)}, u32[]{:S(2)}) collective-permute-start(f32[64,512]{1,0:T(8,128)S(1)} %fusion.182), channel_id=1, source_target_pairs={{16,0},{17,1},{18,2},{19,3},{20,4},{21,5},{22,6},{23,7},{24,8},{25... | collective-permute-start | bytes 393224 | tf_op jit(solution)/shard_map/ppermute | solution.py:35
  523.9 20.1 %collective-permute-start.27 = (bf16[4,4,64,512]{3,2,1,0:T(8,128)(2,1)}, bf16[4,4,64,512]{3,2,1,0:T(8,128)(2,1)}, u32[]{:S(2)}, u32[]{:S(2)}) collective-permute-start(bf16[4,4,64,512]{3,2,1,0:T(8,128)(2,1)} %get-tuple-element.156), channel_id=1, source_target_pairs={{1,0},{0,1},{3,2},{2,3},{5,4},{4,5},{7,6},{6,7},{9,8},{8,9},{11,10... | collective-permute-start | bytes 3145736 | tf_op jit(solution)/shard_map/ppermute | solution.py:35
  531.8 15.9 %all-to-all-start.16 = ((f32[4,32,2048]{2,1,0:T(8,128)}), f32[4,32,2048]{2,1,0:T(8,128)S(1)}, u32[]{:S(2)}, u32[]{:S(2)}) async-start(f32[4,32,2048]{2,1,0:T(8,128)} %broadcast_in_dim.94), calls=%async_computation.16 | async-start | bytes 2097152 | tf_op jit(solution)/shard_map/all_to_all | solution.py:78
  557.9 15.2 %all-to-all-start.18 = ((bf16[4,256,512]{2,1,0:T(8,128)(2,1)}), bf16[4,256,512]{2,1,0:T(8,128)(2,1)S(1)}, u32[]{:S(2)}, u32[]{:S(2)}) async-start(bf16[4,256,512]{2,1,0:T(8,128)(2,1)} %bitcast.106), calls=%async_computation.18 | async-start | bytes 2097152 | tf_op jit(solution)/shard_map/all_to_all | solution.py:369
  (110 other events, 1373.8 us)
Sparse Core Ops, SparseCore 0:
  12.7 87.9 all-gather.2
  102.9 76.1 all-gather.4
  452.5 111.5 reduce-scatter.6
  568.4 114.4 reduce-scatter.8
